TPU v7x, 32 devices: a whole 2x2x4 slice. The times are simulated.
32 devices in a mesh: hb: 4 (over x, core), wb: 2 (over y), hd: 4 (over z).
Axes of the slice: x: 2, y: 2, z: 4, core: 2. Of those that a mesh axis runs over, the one named last changes fastest.
Arguments:
- query_rows: bfloat16 [12, 4, 4, 64, 128], P('hd', 'hb', 'wb'), may hold values from -180 to 180
- key_rows: bfloat16 [12, 4, 4, 64, 128], P('hd', 'hb', 'wb'), may hold values from -6 to 6
- value_rows: bfloat16 [12, 4, 4, 64, 128], P('hd', 'hb', 'wb'), may hold values from -6 to 6
- grad_out: bfloat16 [12, 4, 4, 64, 128], P('hd', 'hb', 'wb'), may hold values from -6 to 6
- sel_tiles: int32 [4, 4, 8], P(None, 'wb'), may hold values from 0 to 7
- sel_count: int32 [4, 4], P(None, 'wb'), may hold values from 1 to 8, as said below
- tile_radius: int32 [12], P('hd'), may hold values from 0 to 1
Outputs:
- grad_query: bfloat16 [12, 4, 4, 64, 128], P('hd', 'hb', 'wb')
- grad_key: bfloat16 [12, 4, 4, 64, 128], P('hd', 'hb', 'wb')
- grad_value: bfloat16 [12, 4, 4, 64, 128], P('hd', 'hb', 'wb')
Inputs may be any that keep to these rules, and one draw needn't show every extreme that they name: sel_count[r, c] is the number of live entries of that query tile's list, from 1 to 8; entries of sel_tiles at positions sel_count or beyond are ignored, and entries may repeat.
All inputs are finite; a program needn't handle non-finite values.
Results may differ from a plain program's by a relative error of at most 0.022.
Values may be sent and summed in bfloat16 or wider, within the bound.
A program may use at most 64 MiB of HBM per device.

v0:
```python
import functools

import jax
import jax.numpy as jnp
from jax import lax
from jax.experimental import pallas as pl
from jax.experimental.pallas import tpu as pltpu
from jax.sharding import PartitionSpec as P

MESH = pl.DeviceIdType.MESH
F32 = jnp.float32
BF16 = jnp.bfloat16
NT = (((1,), (1,)), ((), ()))
NN = (((1,), (0,)), ((), ()))
TN = (((0,), (0,)), ((), ()))


def dot(a, b, dims):
    return lax.dot_general(a, b, dims, preferred_element_type=F32)


def kernel(
    dims,
    q_hbm, k_hbm, v_hbm, g_hbm, sel_hbm, count_hbm, radius_hbm,
    out_ref,
    sel_ref, count_ref, radius_ref, qg, kv, acc_own, acc_chip, tx_sib, rx_sib, tx_chip, rx_chip, tx_edge, rx_edge,
    i_sem, q_sem, kv_sem, s_kvsib, r_kvsib, s_kvchip, r_kvchip, s_relay, r_relay, s_kvedge, r_kvedge,
    s_psib, r_psib, s_pchip, r_pchip, s_pedge, r_pedge,
):
    heads, trows, tcols, tile, picks, n_hb, n_wb, factor = dims
    rows = trows * tcols * tile
    chips = n_hb // 2
    me = lax.axis_index("hb")
    w = lax.axis_index("wb")
    chip, core = me // 2, me % 2
    sib = chip * 2 + 1 - core
    near_rows = 2 * rows + min(2, n_wb - 1) * trows * tile
    to_chip = {j: ((chip + j) % chips) * 2 + core for j in range(1, chips)}
    from_chip = {j: ((chip + chips - j) % chips) * 2 + core for j in range(1, chips)}
    if n_wb == 1:
        links = []
    elif n_wb == 2:
        links = [(None, 1 - w, 0, 0, (1 - w) * (tcols - 1))]
    else:
        links = [(w > 0, w - 1, 0, 1, 0), (w < n_wb - 1, w + 1, 1, 0, tcols - 1)]

    def guarded(there, fn):
        if there is None:
            fn()
        else:
            pl.when(there)(fn)

    def remote(src, dst, send, recv, axis, to):
        return pltpu.make_async_remote_copy(
            src_ref=src, dst_ref=dst, send_sem=send, recv_sem=recv,
            device_id={axis: to}, device_id_type=MESH,
        )

    own_kv = []
    for h in range(heads):
        own_kv.append((
            pltpu.make_async_copy(k_hbm.at[h], kv.at[0, h, pl.ds(0, rows)], kv_sem.at[h, 0]),
            pltpu.make_async_copy(v_hbm.at[h], kv.at[1, h, pl.ds(0, rows)], kv_sem.at[h, 1]),
        ))
        for c in own_kv[-1]:
            c.start()
    own_q = [
        pltpu.make_async_copy(q_hbm, qg.at[0], q_sem.at[0]),
        pltpu.make_async_copy(g_hbm, qg.at[1], q_sem.at[1]),
    ]
    indices = [
        pltpu.make_async_copy(src, dst, i_sem.at[i])
        for i, (src, dst) in enumerate(
            ((sel_hbm, sel_ref), (count_hbm, count_ref), (radius_hbm, radius_ref)))
    ]
    for c in own_q + indices:
        c.start()

    barrier = pltpu.get_barrier_semaphore()
    pl.semaphore_signal(barrier, inc=1, device_id={"hb": sib}, device_id_type=MESH)
    for j in range(1, chips):
        pl.semaphore_signal(barrier, inc=1, device_id={"hb": to_chip[j]}, device_id_type=MESH)
    for there, peer, _, _, _ in links:
        def hello(peer=peer):
            pl.semaphore_signal(barrier, inc=1, device_id={"wb": peer}, device_id_type=MESH)
        guarded(there, hello)
    if n_wb > 2:
        for slot, (there, _, _, _, _) in enumerate(links):
            def blank(slot=slot):
                at = 2 * rows + slot * trows * tile
                kv[:, :, pl.ds(at, trows * tile), :] = jnp.zeros(
                    (2, heads, trows * tile, kv.shape[-1]), BF16)
            pl.when(jnp.logical_not(there))(blank)
    greeted = chips
    for there, _, _, _, _ in links:
        greeted = greeted + (1 if there is None else jnp.where(there, 1, 0))
    pl.semaphore_wait(barrier, greeted)

    def slot_at(s):
        return pl.ds(s * rows if s < 2 else near_rows + (s - 2) * rows, rows)

    def edge_at(slot, r):
        return pl.ds(2 * rows + (slot * trows + r) * tile, tile)

    def kv_chip(h, j, i):
        return remote((k_hbm, v_hbm)[i].at[h], kv.at[i, h, slot_at(2 * j)],
                      s_kvchip.at[h, j, i], r_kvchip.at[h, j, i], "hb", to_chip[j])

    def kv_sib(h):
        return remote(kv.at[:, h, slot_at(0)], kv.at[:, h, slot_at(1)],
                      s_kvsib.at[h], r_kvsib.at[h], "hb", sib)

    def relay(h, j):
        return remote(kv.at[:, h, slot_at(2 * j)], kv.at[:, h, slot_at(2 * j + 1)],
                      s_relay.at[h, j], r_relay.at[h, j], "hb", sib)

    def own_tile(r, col):
        return pl.ds(pl.multiple_of((r * tcols + col) * tile, tile), tile)

    def kv_edge(h, link, r, arriving=False):
        _, peer, here, away, col = link
        slot = here if arriving else away
        return remote(kv.at[:, h, own_tile(r, col)], kv.at[:, h, edge_at(slot, r)],
                      s_kvedge.at[h, away, r], r_kvedge.at[h, slot, r], "wb", peer)

    def p_sib(h, j):
        return remote(tx_sib.at[h, j], rx_sib.at[h, j], s_psib.at[h, j], r_psib.at[h, j], "hb", sib)

    def p_chip(h, j):
        return remote(tx_chip.at[h, j], rx_chip.at[h, j],
                      s_pchip.at[h, j], r_pchip.at[h, j], "hb", from_chip[j])

    def p_edge(h, link, arriving=False):
        _, peer, here, away, _ = link
        slot = here if arriving else away
        return remote(tx_edge.at[h, here], rx_edge.at[h, slot],
                      s_pedge.at[h, here], r_pedge.at[h, slot], "wb", peer)

    for h in range(heads):
        for j in range(1, chips):
            for i in range(2):
                kv_chip(h, j, i).start()
    for h in range(heads):
        for c in own_kv[h]:
            c.wait()
        kv_sib(h).start()
        for link in links:
            def send(link=link, h=h):
                for r in range(trows):
                    kv_edge(h, link, r).start()
            guarded(link[0], send)

    for c in indices:
        c.wait()
    lane_tile = lax.broadcasted_iota(jnp.int32, (1, rows), 1) // tile
    lane_row = me * trows + lane_tile // tcols
    lane_col = lane_tile % tcols
    chosen = []
    for s in range(picks):
        entry = jnp.full((1, rows), -1, jnp.int32)
        for r in range(trows):
            for c in range(tcols):
                row = me * trows + r
                value = jnp.where(s < count_ref[c, row], sel_ref[row, c, s], -1)
                entry = jnp.where(lane_tile == r * tcols + c, value, entry)
        chosen.append(entry)
    spread, picked = [], []
    for s in range(n_hb):
        j = s // 2
        group = ((chip + chips - j) % chips) * 2 + (core if s % 2 == 0 else 1 - core)
        for r in range(trows):
            for c in range(tcols):
                key_row = group * trows + r
                spread.append(jnp.abs(lane_row - key_row) + jnp.abs(lane_col - c))
                at = key_row * tcols + c
                hit = functools.reduce(jnp.logical_or, [e == at for e in chosen])
                picked.append(hit)
    beside = []
    for there, _, slot, _, col in links:
        for r in range(trows):
            near = lane_tile == r * tcols + col
            if there is not None:
                near = jnp.logical_and(near, there)
            beside.append(near)

    for c in own_q:
        c.wait()

    near_tiles = 2 * trows * tcols

    def products(h, at):
        return dot(kv[0, h, at], qg[0, h], NT), dot(kv[1, h, at], qg[1, h], NT)

    def near_products(h):
        kv_sib(h).wait_recv()
        for link in links:
            def arrive(link=link):
                for r in range(trows):
                    kv_edge(h, link, r, True).wait_recv()
            guarded(link[0], arrive)
        return products(h, slice(0, near_rows))

    def softmax(h, blocks):
        radius = radius_ref[h]
        bias = [jnp.where(jnp.logical_or(sp <= radius, pk), 0.0, -jnp.inf)
                for sp, pk in zip(spread, picked)]
        edge = [jnp.where(jnp.logical_and(near, radius >= 1), 0.0, -jnp.inf) for near in beside]
        bias = bias[:near_tiles] + edge + bias[near_tiles:]
        s_t, d_t = [], []
        for scores, slopes in blocks:
            for i in range(scores.shape[0] // tile):
                cut = slice(i * tile, (i + 1) * tile)
                s_t.append(scores[cut] * factor + bias[len(s_t)])
                d_t.append(slopes[cut])
        top = jnp.max(functools.reduce(jnp.maximum, s_t), axis=0, keepdims=True)
        e_t = [jnp.exp(s - top) for s in s_t]
        total = jnp.sum(functools.reduce(jnp.add, e_t), axis=0, keepdims=True)
        mixed = jnp.sum(functools.reduce(jnp.add, [e * d for e, d in zip(e_t, d_t)]),
                        axis=0, keepdims=True)
        inverse = 1.0 / total
        delta = mixed * inverse
        probs = [e * inverse for e in e_t]
        half = jnp.concatenate([p.astype(BF16) for p in probs], axis=0)
        grad = jnp.concatenate(
            [(p * ((d - delta) * factor)).astype(BF16) for p, d in zip(probs, d_t)], axis=0)
        return half, grad

    def pass_on(h):
        for j in range(1, chips):
            for i in range(2):
                kv_chip(h, j, i).wait_recv()
            relay(h, j).start()

    blocks = [near_products(0)]
    pass_on(0)
    for h in range(heads):
        if chips > 1:
            for j in range(1, chips):
                relay(h, j).wait_recv()
            blocks.append(products(h, slice(near_rows, near_rows + (n_hb - 2) * rows)))
        half, grad = softmax(h, blocks)
        q, g = qg[0, h], qg[1, h]
        if chips > 1:
            far_parts = (dot(grad[near_rows:], q, NN), dot(half[near_rows:], g, NN))
            for j in range(1, chips):
                at = (2 * j - 2) * rows
                for i, part in enumerate(far_parts):
                    tx_sib[h, j, i] = part[at + rows:at + 2 * rows].astype(BF16)
                    acc_chip[h, j, i] = part[at:at + rows]
                p_sib(h, j).start()
        if h + 1 < heads:
            pass_on(h + 1)
        near_parts = (dot(grad[:near_rows], q, NN), dot(half[:near_rows], g, NN))
        for i, part in enumerate(near_parts):
            tx_sib[h, 0, i] = part[rows:2 * rows].astype(BF16)
            acc_own[h, i] = part[:rows]
        p_sib(h, 0).start()
        for link in links:
            at = 2 * rows + link[2] * trows * tile
            for i, part in enumerate(near_parts):
                tx_edge[h, link[2], i] = part[at:at + trows * tile].astype(BF16)
            guarded(link[0], lambda link=link, h=h: p_edge(h, link).start())
        out_ref[0, h] = dot(grad, kv[0, h], TN).astype(BF16)
        if h + 1 < heads:
            blocks = [near_products(h + 1)]
        for j in range(1, chips):
            p_sib(h, j).wait_recv()
            for i in range(2):
                tx_chip[h, j, i] = (acc_chip[h, j, i] + rx_sib[h, j, i].astype(F32)).astype(BF16)
            p_chip(h, j).start()

    for h in range(heads):
        p_sib(h, 0).wait_recv()
        for link in links:
            there, _, here, _, col = link

            def add_edge(link=link, here=here, col=col, h=h):
                p_edge(h, link, True).wait_recv()
                for i in range(2):
                    for r in range(trows):
                        at = own_tile(r, col)
                        acc_own[h, i, at] += rx_edge[h, here, i, pl.ds(r * tile, tile)].astype(F32)
            guarded(there, add_edge)
        totals = [acc_own[h, i] + rx_sib[h, 0, i].astype(F32) for i in range(2)]
        for j in range(1, chips):
            p_chip(h, j).wait_recv()
            for i in range(2):
                totals[i] = totals[i] + rx_chip[h, j, i].astype(F32)
        out_ref[1, h] = totals[0].astype(BF16)
        out_ref[2, h] = totals[1].astype(BF16)

    for h in range(heads):
        kv_sib(h).wait_send()
        p_sib(h, 0).wait_send()
        for j in range(1, chips):
            for i in range(2):
                kv_chip(h, j, i).wait_send()
            relay(h, j).wait_send()
            p_sib(h, j).wait_send()
            p_chip(h, j).wait_send()
        for link in links:
            def drain(link=link, h=h):
                for r in range(trows):
                    kv_edge(h, link, r).wait_send()
                p_edge(h, link).wait_send()
            guarded(link[0], drain)


def unstack(stacked, dq_hbm, dk_hbm, dv_hbm, sem):
    copies = [pltpu.make_async_copy(stacked.at[i], out, sem.at[i])
              for i, out in enumerate((dq_hbm, dk_hbm, dv_hbm))]
    for c in copies:
        c.start()
    for c in copies:
        c.wait()


def on_device(n_hb, n_wb, query_rows, key_rows, value_rows, grad_out, sel_tiles, sel_count, tile_radius):
    heads, trows, tcols, tile, depth = query_rows.shape
    picks = sel_tiles.shape[-1]
    rows = trows * tcols * tile
    chips = n_hb // 2
    sides = max(1, min(2, n_wb - 1))
    used = min(2, n_wb - 1)
    flat = (heads, rows, depth)
    keys = n_hb * rows + used * trows * tile
    dma = pltpu.SemaphoreType.DMA
    dims = (heads, trows, tcols, tile, picks, n_hb, n_wb, depth ** -0.5)
    hbm = pl.BlockSpec(memory_space=pltpu.HBM)
    vmem = pl.BlockSpec(memory_space=pltpu.VMEM)
    out = jax.ShapeDtypeStruct(flat, BF16)
    stacked = pl.pallas_call(
        functools.partial(kernel, dims),
        out_shape=pltpu.VMEM((3,) + flat, BF16),
        in_specs=[hbm] * 7,
        out_specs=vmem,
        scratch_shapes=[
            pltpu.SMEM(sel_tiles.shape, jnp.int32),
            pltpu.SMEM(sel_count.shape[::-1], jnp.int32),
            pltpu.SMEM(tile_radius.shape, jnp.int32),
            pltpu.VMEM((2,) + flat, BF16),
            pltpu.VMEM((2, heads, keys, depth), BF16),
            pltpu.VMEM((heads, 2, rows, depth), F32),
            pltpu.VMEM((heads, chips, 2, rows, depth), F32),
            pltpu.VMEM((heads, chips, 2, rows, depth), BF16),
            pltpu.VMEM((heads, chips, 2, rows, depth), BF16),
            pltpu.VMEM((heads, chips, 2, rows, depth), BF16),
            pltpu.VMEM((heads, chips, 2, rows, depth), BF16),
            pltpu.VMEM((heads, sides, 2, trows * tile, depth), BF16),
            pltpu.VMEM((heads, sides, 2, trows * tile, depth), BF16),
            dma((3,)), dma((2,)), dma((heads, 2)),
            dma((heads,)), dma((heads,)),
            dma((heads, chips, 2)), dma((heads, chips, 2)),
            dma((heads, chips)), dma((heads, chips)),
            dma((heads, sides, trows)), dma((heads, sides, trows)),
            dma((heads, chips)), dma((heads, chips)),
            dma((heads, chips)), dma((heads, chips)),
            dma((heads, sides)), dma((heads, sides)),
        ],
        compiler_params=pltpu.CompilerParams(
            collective_id=0, has_side_effects=True, vmem_limit_bytes=62 * 1024 * 1024),
        cost_estimate=pl.CostEstimate(
            flops=10 * heads * rows * keys * depth,
            bytes_accessed=14 * heads * rows * depth,
            transcendentals=heads * rows * keys),
    )(
        query_rows.reshape(flat), key_rows.reshape(flat), value_rows.reshape(flat),
        grad_out.reshape(flat), sel_tiles, sel_count.T, tile_radius,
    )
    results = pl.pallas_call(
        unstack,
        out_shape=(out, out, out),
        in_specs=[vmem],
        out_specs=(hbm,) * 3,
        scratch_shapes=[dma((3,))],
        compiler_params=pltpu.CompilerParams(vmem_limit_bytes=1024 * 1024),
    )(stacked)
    return tuple(r.reshape(query_rows.shape) for r in results)


def solution(mesh):
    block = P("hd", "hb", "wb", None, None)
    return jax.shard_map(
        functools.partial(on_device, mesh.shape["hb"], mesh.shape["wb"]),
        mesh=mesh,
        in_specs=(block, block, block, block, P(None, "wb", None), P(None, "wb"), P("hd")),
        out_specs=(block, block, block),
        check_vma=False,
    )
```

profile of v0, /device:TPU:0, one launch (start us, length us, event | category | flops | bytes accessed | tf_op | source)
XLA Modules:
  0.0 18.4 jit_solution(5804544410841882390)
XLA Ops:
  0.6 17.0 %shard_map.94.stacked = bf16[3,3,128,128]{3,2,1,0:T(8,128)(2,1)S(1)} custom-call(bf16[3,128,128]{2,1,0:T(8,128)(2,1)} %bitcast.14, bf16[3,128,128]{2,1,0:T(8,128)(2,1)} %bitcast.15, bf16[3,128,128]{2,1,0:T(8,128)(2,1)} %bitcast.16, bf16[3,128,128]{2,1,0:T(8,128)(2,1)} %bitcast.17, s32[4,2,8]{2,1,0:T(2,128)} %sel_hbm.1, s32[2,4]{1,0:T(2,128)} %bitcast.21, ...), custom_call_target="tpu_custom_call" | custom-call | flops 283115520 | bytes 688128 | tf_op jit(solution)/shard_map/pallas_call | solution.py:332
  17.7 0.7 %shard_map.95 = (bf16[3,128,128]{2,1,0:T(8,128)(2,1)}, bf16[3,128,128]{2,1,0:T(8,128)(2,1)}, bf16[3,128,128]{2,1,0:T(8,128)(2,1)}) custom-call(bf16[3,3,128,128]{3,2,1,0:T(8,128)(2,1)S(1)} %shard_map.94.stacked), custom_call_target="tpu_custom_call" | custom-call | tf_op jit(solution)/shard_map/pallas_call | solution.py:370
where the time goes:
time: 18.6 us; the launch traced here: 18.4 us
  Pallas kernels  17.8 us (96%)
  between operations  0.64 us (3%)
    pallas_call x1, Pallas kernels, on_device(): pl.pallas_call(functools.partial(kernel, dims), out_shape=pltpu.VMEM((3,)...  17 us
    pallas_call x1, Pallas kernels, on_device(): pl.pallas_call(unstack, out_shape=(out, out, out), in_specs=[vmem], out_s...  0.73 us

commit v1 on v0

--- a/solution.py
+++ b/solution.py
@@ -136,10 +136,14 @@
         return remote(tx_edge.at[h, here], rx_edge.at[h, slot],
                       s_pedge.at[h, here], r_pedge.at[h, slot], "wb", peer)
 
-    for h in range(heads):
+    def send_chip(h):
         for j in range(1, chips):
             for i in range(2):
+                if h:
+                    kv_chip(h - 1, j, i).wait_send()
                 kv_chip(h, j, i).start()
+
+    send_chip(0)
     for h in range(heads):
         for c in own_kv[h]:
             c.wait()
@@ -232,8 +236,12 @@
             relay(h, j).start()
 
     blocks = [near_products(0)]
+    if heads > 1:
+        send_chip(1)
     pass_on(0)
     for h in range(heads):
+        if h + 2 < heads:
+            send_chip(h + 2)
         if chips > 1:
             for j in range(1, chips):
                 relay(h, j).wait_recv()
@@ -293,8 +301,9 @@
         kv_sib(h).wait_send()
         p_sib(h, 0).wait_send()
         for j in range(1, chips):
-            for i in range(2):
-                kv_chip(h, j, i).wait_send()
+            if h == heads - 1:
+                for i in range(2):
+                    kv_chip(h, j, i).wait_send()
             relay(h, j).wait_send()
             p_sib(h, j).wait_send()
             p_chip(h, j).wait_send()

time: 18.6 us -> 20.1 us (1.081)
  Pallas kernels: 17.8 us -> 19.3 us
    pallas_call x1, Pallas kernels: 17 us -> 18.5 us  [on_device(): pl.pallas_call(functools.partial(kernel, dims), out_shape=pltpu.VMEM((3,)...]
where the time goes in v1:
time: 20.1 us; the launch traced here: 19.9 us
  Pallas kernels  19.3 us (96%)
  between operations  0.64 us (3%)
    pallas_call x1, Pallas kernels, on_device(): pl.pallas_call(functools.partial(kernel, dims), out_shape=pltpu.VMEM((3,)...  18.5 us
    pallas_call x1, Pallas kernels, on_device(): pl.pallas_call(unstack, out_shape=(out, out, out), in_specs=[vmem], out_s...  0.73 us

profile of v1, /device:TPU:0, one launch (start us, length us, event | category | flops | bytes accessed | tf_op | source)
XLA Modules:
  0.0 19.9 jit_solution(15766633386119074157)
XLA Ops:
  0.6 18.5 %shard_map.94.stacked = bf16[3,3,128,128]{3,2,1,0:T(8,128)(2,1)S(1)} custom-call(bf16[3,128,128]{2,1,0:T(8,128)(2,1)} %bitcast.14, bf16[3,128,128]{2,1,0:T(8,128)(2,1)} %bitcast.15, bf16[3,128,128]{2,1,0:T(8,128)(2,1)} %bitcast.16, bf16[3,128,128]{2,1,0:T(8,128)(2,1)} %bitcast.17, s32[4,2,8]{2,1,0:T(2,128)} %sel_hbm.1, s32[2,4]{1,0:T(2,128)} %bitcast.21, ...), custom_call_target="tpu_custom_call" | custom-call | flops 283115520 | bytes 688128 | tf_op jit(solution)/shard_map/pallas_call | solution.py:341
  19.2 0.7 %shard_map.95 = (bf16[3,128,128]{2,1,0:T(8,128)(2,1)}, bf16[3,128,128]{2,1,0:T(8,128)(2,1)}, bf16[3,128,128]{2,1,0:T(8,128)(2,1)}) custom-call(bf16[3,3,128,128]{3,2,1,0:T(8,128)(2,1)S(1)} %shard_map.94.stacked), custom_call_target="tpu_custom_call" | custom-call | tf_op jit(solution)/shard_map/pallas_call | solution.py:379

commit v2 on v0

--- a/solution.py
+++ b/solution.py
@@ -110,9 +110,9 @@
         return remote(kv.at[:, h, slot_at(0)], kv.at[:, h, slot_at(1)],
                       s_kvsib.at[h], r_kvsib.at[h], "hb", sib)
 
-    def relay(h, j):
-        return remote(kv.at[:, h, slot_at(2 * j)], kv.at[:, h, slot_at(2 * j + 1)],
-                      s_relay.at[h, j], r_relay.at[h, j], "hb", sib)
+    def relay(h, j, i):
+        return remote(kv.at[i, h, slot_at(2 * j)], kv.at[i, h, slot_at(2 * j + 1)],
+                      s_relay.at[h, j, i], r_relay.at[h, j, i], "hb", sib)
 
     def own_tile(r, col):
         return pl.ds(pl.multiple_of((r * tcols + col) * tile, tile), tile)
@@ -123,12 +123,13 @@
         return remote(kv.at[:, h, own_tile(r, col)], kv.at[:, h, edge_at(slot, r)],
                       s_kvedge.at[h, away, r], r_kvedge.at[h, slot, r], "wb", peer)
 
-    def p_sib(h, j):
-        return remote(tx_sib.at[h, j], rx_sib.at[h, j], s_psib.at[h, j], r_psib.at[h, j], "hb", sib)
-
-    def p_chip(h, j):
-        return remote(tx_chip.at[h, j], rx_chip.at[h, j],
-                      s_pchip.at[h, j], r_pchip.at[h, j], "hb", from_chip[j])
+    def p_sib(h, j, i):
+        return remote(tx_sib.at[h, j, i], rx_sib.at[h, j, i],
+                      s_psib.at[h, j, i], r_psib.at[h, j, i], "hb", sib)
+
+    def p_chip(h, j, i):
+        return remote(tx_chip.at[h, j, i], rx_chip.at[h, j, i],
+                      s_pchip.at[h, j, i], r_pchip.at[h, j, i], "hb", from_chip[j])
 
     def p_edge(h, link, arriving=False):
         _, peer, here, away, _ = link
@@ -188,8 +189,8 @@
 
     near_tiles = 2 * trows * tcols
 
-    def products(h, at):
-        return dot(kv[0, h, at], qg[0, h], NT), dot(kv[1, h, at], qg[1, h], NT)
+    def product(i, h, at):
+        return dot(kv[i, h, at], qg[i, h], NT)
 
     def near_products(h):
         kv_sib(h).wait_recv()
@@ -198,7 +199,7 @@
                 for r in range(trows):
                     kv_edge(h, link, r, True).wait_recv()
             guarded(link[0], arrive)
-        return products(h, slice(0, near_rows))
+        return [product(i, h, slice(0, near_rows)) for i in range(2)]
 
     def softmax(h, blocks):
         radius = radius_ref[h]
@@ -226,35 +227,38 @@
         return half, grad
 
     def pass_on(h):
-        for j in range(1, chips):
-            for i in range(2):
+        for i in range(2):
+            for j in range(1, chips):
                 kv_chip(h, j, i).wait_recv()
-            relay(h, j).start()
+                relay(h, j, i).start()
 
     blocks = [near_products(0)]
     pass_on(0)
     for h in range(heads):
         if chips > 1:
-            for j in range(1, chips):
-                relay(h, j).wait_recv()
-            blocks.append(products(h, slice(near_rows, near_rows + (n_hb - 2) * rows)))
+            far = []
+            for i in range(2):
+                for j in range(1, chips):
+                    relay(h, j, i).wait_recv()
+                far.append(product(i, h, slice(near_rows, near_rows + (n_hb - 2) * rows)))
+            blocks.append(far)
         half, grad = softmax(h, blocks)
         q, g = qg[0, h], qg[1, h]
         if chips > 1:
-            far_parts = (dot(grad[near_rows:], q, NN), dot(half[near_rows:], g, NN))
-            for j in range(1, chips):
-                at = (2 * j - 2) * rows
-                for i, part in enumerate(far_parts):
+            for i in (1, 0):
+                part = dot((grad, half)[i][near_rows:], (q, g)[i], NN)
+                for j in range(1, chips):
+                    at = (2 * j - 2) * rows
                     tx_sib[h, j, i] = part[at + rows:at + 2 * rows].astype(BF16)
                     acc_chip[h, j, i] = part[at:at + rows]
-                p_sib(h, j).start()
+                    p_sib(h, j, i).start()
         if h + 1 < heads:
             pass_on(h + 1)
         near_parts = (dot(grad[:near_rows], q, NN), dot(half[:near_rows], g, NN))
         for i, part in enumerate(near_parts):
             tx_sib[h, 0, i] = part[rows:2 * rows].astype(BF16)
             acc_own[h, i] = part[:rows]
-        p_sib(h, 0).start()
+            p_sib(h, 0, i).start()
         for link in links:
             at = 2 * rows + link[2] * trows * tile
             for i, part in enumerate(near_parts):
@@ -263,14 +267,15 @@
         out_ref[0, h] = dot(grad, kv[0, h], TN).astype(BF16)
         if h + 1 < heads:
             blocks = [near_products(h + 1)]
-        for j in range(1, chips):
-            p_sib(h, j).wait_recv()
-            for i in range(2):
+        for i in (1, 0):
+            for j in range(1, chips):
+                p_sib(h, j, i).wait_recv()
                 tx_chip[h, j, i] = (acc_chip[h, j, i] + rx_sib[h, j, i].astype(F32)).astype(BF16)
-            p_chip(h, j).start()
-
-    for h in range(heads):
-        p_sib(h, 0).wait_recv()
+                p_chip(h, j, i).start()
+
+    for h in range(heads):
+        for i in range(2):
+            p_sib(h, 0, i).wait_recv()
         for link in links:
             there, _, here, _, col = link
 
@@ -282,22 +287,19 @@
                         acc_own[h, i, at] += rx_edge[h, here, i, pl.ds(r * tile, tile)].astype(F32)
             guarded(there, add_edge)
         totals = [acc_own[h, i] + rx_sib[h, 0, i].astype(F32) for i in range(2)]
-        for j in range(1, chips):
-            p_chip(h, j).wait_recv()
-            for i in range(2):
+        for i in (1, 0):
+            for j in range(1, chips):
+                p_chip(h, j, i).wait_recv()
                 totals[i] = totals[i] + rx_chip[h, j, i].astype(F32)
-        out_ref[1, h] = totals[0].astype(BF16)
-        out_ref[2, h] = totals[1].astype(BF16)
+            out_ref[1 + i, h] = totals[i].astype(BF16)
 
     for h in range(heads):
         kv_sib(h).wait_send()
-        p_sib(h, 0).wait_send()
-        for j in range(1, chips):
-            for i in range(2):
-                kv_chip(h, j, i).wait_send()
-            relay(h, j).wait_send()
-            p_sib(h, j).wait_send()
-            p_chip(h, j).wait_send()
+        for i in range(2):
+            p_sib(h, 0, i).wait_send()
+            for j in range(1, chips):
+                for copy in (kv_chip, relay, p_sib, p_chip):
+                    copy(h, j, i).wait_send()
         for link in links:
             def drain(link=link, h=h):
                 for r in range(trows):
@@ -351,10 +353,10 @@
             dma((3,)), dma((2,)), dma((heads, 2)),
             dma((heads,)), dma((heads,)),
             dma((heads, chips, 2)), dma((heads, chips, 2)),
-            dma((heads, chips)), dma((heads, chips)),
+            dma((heads, chips, 2)), dma((heads, chips, 2)),
             dma((heads, sides, trows)), dma((heads, sides, trows)),
-            dma((heads, chips)), dma((heads, chips)),
-            dma((heads, chips)), dma((heads, chips)),
+            dma((heads, chips, 2)), dma((heads, chips, 2)),
+            dma((heads, chips, 2)), dma((heads, chips, 2)),
             dma((heads, sides)), dma((heads, sides)),
         ],
         compiler_params=pltpu.CompilerParams(

time: 18.6 us -> 18.6 us (level)
  no operation moved by 1% of the time
where the time goes in v2:
time: 18.6 us; the launch traced here: 18.5 us
  Pallas kernels  17.8 us (96%)
  between operations  0.64 us (3%)
    pallas_call x1, Pallas kernels, on_device(): pl.pallas_call(functools.partial(kernel, dims), out_shape=pltpu.VMEM((3,)...  17.1 us
    pallas_call x1, Pallas kernels, on_device(): pl.pallas_call(unstack, out_shape=(out, out, out), in_specs=[vmem], out_s...  0.73 us

profile of v2, /device:TPU:0, one launch (start us, length us, event | category | flops | bytes accessed | tf_op | source)
XLA Modules:
  0.0 18.5 jit_solution(15465570920116580563)
XLA Ops:
  0.6 17.1 %shard_map.94.stacked = bf16[3,3,128,128]{3,2,1,0:T(8,128)(2,1)S(1)} custom-call(bf16[3,128,128]{2,1,0:T(8,128)(2,1)} %bitcast.14, bf16[3,128,128]{2,1,0:T(8,128)(2,1)} %bitcast.15, bf16[3,128,128]{2,1,0:T(8,128)(2,1)} %bitcast.16, bf16[3,128,128]{2,1,0:T(8,128)(2,1)} %bitcast.17, s32[4,2,8]{2,1,0:T(2,128)} %sel_hbm.1, s32[2,4]{1,0:T(2,128)} %bitcast.21, ...), custom_call_target="tpu_custom_call" | custom-call | flops 283115520 | bytes 688128 | tf_op jit(solution)/shard_map/pallas_call | solution.py:334
  17.7 0.7 %shard_map.95 = (bf16[3,128,128]{2,1,0:T(8,128)(2,1)}, bf16[3,128,128]{2,1,0:T(8,128)(2,1)}, bf16[3,128,128]{2,1,0:T(8,128)(2,1)}) custom-call(bf16[3,3,128,128]{3,2,1,0:T(8,128)(2,1)S(1)} %shard_map.94.stacked), custom_call_target="tpu_custom_call" | custom-call | tf_op jit(solution)/shard_map/pallas_call | solution.py:372

commit v3 on v2

--- a/solution.py
+++ b/solution.py
@@ -137,10 +137,12 @@
         return remote(tx_edge.at[h, here], rx_edge.at[h, slot],
                       s_pedge.at[h, here], r_pedge.at[h, slot], "wb", peer)
 
-    for h in range(heads):
+    def send_chip(h):
         for j in range(1, chips):
             for i in range(2):
                 kv_chip(h, j, i).start()
+
+    send_chip(0)
     for h in range(heads):
         for c in own_kv[h]:
             c.wait()
@@ -151,6 +153,8 @@
                     kv_edge(h, link, r).start()
             guarded(link[0], send)
 
+    if heads > 1:
+        send_chip(1)
     for c in indices:
         c.wait()
     lane_tile = lax.broadcasted_iota(jnp.int32, (1, rows), 1) // tile
@@ -233,6 +237,8 @@
                 relay(h, j, i).start()
 
     blocks = [near_products(0)]
+    for h in range(2, heads):
+        send_chip(h)
     pass_on(0)
     for h in range(heads):
         if chips > 1:

time: 18.6 us -> 18.2 us (0.978)
  Pallas kernels: 17.8 us -> 17.4 us
    pallas_call x1, Pallas kernels: 17.1 us -> 16.7 us  [on_device(): pl.pallas_call(functools.partial(kernel, dims), out_shape=pltpu.VMEM((3,)...]
where the time goes in v3:
time: 18.2 us; the launch traced here: 18 us
  Pallas kernels  17.4 us (96%)
  between operations  0.64 us (4%)
    pallas_call x1, Pallas kernels, on_device(): pl.pallas_call(functools.partial(kernel, dims), out_shape=pltpu.VMEM((3,)...  16.7 us
    pallas_call x1, Pallas kernels, on_device(): pl.pallas_call(unstack, out_shape=(out, out, out), in_specs=[vmem], out_s...  0.73 us

profile of v3, /device:TPU:0, one launch (start us, length us, event | category | flops | bytes accessed | tf_op | source)
XLA Modules:
  0.0 18.0 jit_solution(10617596956042715957)
XLA Ops:
  0.6 16.7 %shard_map.94.stacked = bf16[3,3,128,128]{3,2,1,0:T(8,128)(2,1)S(1)} custom-call(bf16[3,128,128]{2,1,0:T(8,128)(2,1)} %bitcast.14, bf16[3,128,128]{2,1,0:T(8,128)(2,1)} %bitcast.15, bf16[3,128,128]{2,1,0:T(8,128)(2,1)} %bitcast.16, bf16[3,128,128]{2,1,0:T(8,128)(2,1)} %bitcast.17, s32[4,2,8]{2,1,0:T(2,128)} %sel_hbm.1, s32[2,4]{1,0:T(2,128)} %bitcast.21, ...), custom_call_target="tpu_custom_call" | custom-call | flops 283115520 | bytes 688128 | tf_op jit(solution)/shard_map/pallas_call | solution.py:340
  17.3 0.7 %shard_map.95 = (bf16[3,128,128]{2,1,0:T(8,128)(2,1)}, bf16[3,128,128]{2,1,0:T(8,128)(2,1)}, bf16[3,128,128]{2,1,0:T(8,128)(2,1)}) custom-call(bf16[3,3,128,128]{3,2,1,0:T(8,128)(2,1)S(1)} %shard_map.94.stacked), custom_call_target="tpu_custom_call" | custom-call | tf_op jit(solution)/shard_map/pallas_call | solution.py:378
